TPU v7x, 32 devices: a whole 2x2x4 slice. The times are simulated.
32 devices in a mesh: grp: 2 (over y), seq: 16 (over z, x, core).
Axes of the slice: x: 2, y: 2, z: 4, core: 2. Of those that a mesh axis runs over, the one named last changes fastest.
Arguments:
- signal: bfloat16 [1024, 4096], P(None, ('grp', 'seq')), parts along dimension 1, may hold values from -6 to 6
- gate: bfloat16 [1024, 4096], P(None, ('grp', 'seq')), parts along dimension 1, may hold values from -6 to 6
- filter_taps: float32 [1024, 2048], P(None, 'seq'), may hold values from -2 to 2
- skip: float32 [1024], replicated, may hold values from -4 to 4
- up1_weight: bfloat16 [1024, 2048], replicated, may hold values from -0.1875 to 0.1875
- up1_bias: float32 [512], replicated, may hold values from -3 to 3
- res1_weight: bfloat16 [3584, 512], replicated, may hold values from -0.09375 to 0.09375
- res1_bias: float32 [512], replicated, may hold values from -3 to 3
- up2_weight: bfloat16 [512, 1024], replicated, may hold values from -0.25 to 0.25
- up2_bias: float32 [256], replicated, may hold values from -3 to 3
- res2_weight: bfloat16 [1792, 256], replicated, may hold values from -0.125 to 0.125
- res2_bias: float32 [256], replicated, may hold values from -3 to 3
- up3_weight: bfloat16 [256, 512], replicated, may hold values from -0.375 to 0.375
- up3_bias: float32 [128], replicated, may hold values from -3 to 3
- res3_weight: bfloat16 [896, 128], replicated, may hold values from -0.1875 to 0.1875
- res3_bias: float32 [128], replicated, may hold values from -3 to 3
Outputs:
- waveform_features: bfloat16 [262144, 128], P(('grp', 'seq')), parts along dimension 0
There are 2 independent parts, one for each index of `grp`. A program takes and returns all parts, laid end to end along the dimension named above; an argument that names none is the same for every part. Nothing has to cross between parts.
All inputs are finite; a program needn't handle non-finite values.
Results may differ from a plain program's by a relative error of at most 0.018.
Values may be sent and summed in bfloat16 or wider, within the bound.
A program may use at most 128 MiB of HBM per device.

v0:
```python
import functools
import math

import jax
import jax.numpy as jnp
from jax import lax
from jax.experimental import pallas as pl
from jax.experimental.pallas import tpu as pltpu
from jax.sharding import PartitionSpec as P

HIGHEST = lax.Precision.HIGHEST


def angle_table(rows, cols, modulus):
    product = (
        lax.broadcasted_iota(jnp.int32, (rows, cols), 0)
        * lax.broadcasted_iota(jnp.int32, (rows, cols), 1)
        % modulus
    )
    theta = product.astype(jnp.float32) * (2.0 * math.pi / modulus)
    return (jnp.cos(theta), jnp.sin(theta))


def forward(values, tables):
    outer_cos, outer_sin, twist_cos, twist_sin, inner_cos, inner_sin = tables
    first_re = jnp.einsum("kn,cnm->ckm", outer_cos, values, precision=HIGHEST)
    first_im = -jnp.einsum("kn,cnm->ckm", outer_sin, values, precision=HIGHEST)
    turned_re = first_re * twist_cos + first_im * twist_sin
    turned_im = first_im * twist_cos - first_re * twist_sin
    spec_re = jnp.einsum("ckm,mj->ckj", turned_re, inner_cos, precision=HIGHEST) + jnp.einsum(
        "ckm,mj->ckj", turned_im, inner_sin, precision=HIGHEST
    )
    spec_im = jnp.einsum("ckm,mj->ckj", turned_im, inner_cos, precision=HIGHEST) - jnp.einsum(
        "ckm,mj->ckj", turned_re, inner_sin, precision=HIGHEST
    )
    return (spec_re, spec_im)


def inverse(spec_re, spec_im, tables, modulus):
    outer_cos, outer_sin, twist_cos, twist_sin, inner_cos, inner_sin = tables
    back_re = jnp.einsum("ckm,mj->ckj", spec_re, inner_cos, precision=HIGHEST) - jnp.einsum(
        "ckm,mj->ckj", spec_im, inner_sin, precision=HIGHEST
    )
    back_im = jnp.einsum("ckm,mj->ckj", spec_im, inner_cos, precision=HIGHEST) + jnp.einsum(
        "ckm,mj->ckj", spec_re, inner_sin, precision=HIGHEST
    )
    turned_re = back_re * twist_cos - back_im * twist_sin
    turned_im = back_im * twist_cos + back_re * twist_sin
    result = jnp.einsum("kn,ckm->cnm", outer_cos, turned_re, precision=HIGHEST) - jnp.einsum(
        "kn,ckm->cnm", outer_sin, turned_im, precision=HIGHEST
    )
    return result / modulus


def gelu(v):
    return 0.5 * v * (1.0 + jnp.tanh(0.7978845608 * (v + 0.044715 * (v * v * v))))


def decoder_kernel(
    frames, edge, lat_ref, b1_ref, rb1_ref, b2_ref, rb2_ref, b3_ref, rb3_ref, edges_ref,
    up1_hbm, res1_hbm, up2_hbm, res2_hbm, up3_hbm, res3_hbm,
    out_ref,
    up1, res1, up2, res2, up3, res3, act1, hid1, x1, act2, hid2, x2, act3, hid3, fine, sems,
):
    copies = [
        pltpu.make_async_copy(src, dst, sems.at[i])
        for i, (src, dst) in enumerate(
            [(up1_hbm, up1), (res1_hbm, res1), (up2_hbm, up2), (res2_hbm, res2), (up3_hbm, up3), (res3_hbm, res3)]
        )
    ]
    for copy in copies:
        copy.start()
    rows = frames + edge
    w1, w2, w3 = b1_ref.shape[1], b2_ref.shape[1], b3_ref.shape[1]
    at = lax.broadcasted_iota(jnp.int32, (rows, 1), 0)
    keep_first = edges_ref[0:1, 0:1]
    keep_last = edges_ref[1:2, 0:1]
    before_scale = jnp.where(at == 0, keep_first, 1.0)
    after_scale = jnp.where(at == frames - 1, keep_last, 1.0)

    def before(v):
        return (pltpu.roll(v, 1, 0) * before_scale).astype(jnp.bfloat16)

    def after(v):
        return (pltpu.roll(v, rows - 1, 0) * after_scale).astype(jnp.bfloat16)

    def dot(a, b):
        return jnp.dot(a, b, preferred_element_type=jnp.float32)

    copies[0].wait()
    for k in range(4):
        h = (dot(lat_ref[...], up1[:, k * w1 : (k + 1) * w1]) + b1_ref[...]).astype(jnp.bfloat16)
        hid1[:, k * w1 : (k + 1) * w1] = h
        a = gelu(h.astype(jnp.float32))
        act1[:, (3 + k) * w1 : (4 + k) * w1] = a.astype(jnp.bfloat16)
        if k > 0:
            act1[:, (k - 1) * w1 : k * w1] = before(a)
        if k < 3:
            act1[:, (7 + k) * w1 : (8 + k) * w1] = after(a)
    copies[1].wait()
    for k in range(4):
        y = dot(act1[:, k * w1 : (k + 7) * w1], res1[...])
        y = y + hid1[:, k * w1 : (k + 1) * w1].astype(jnp.float32) + rb1_ref[...]
        x1[k * rows : (k + 1) * rows, :] = y.astype(jnp.bfloat16)

    def section(blocks, x, up, up_bias, hid, act, w, group):
        @pl.loop(0, blocks)
        def _(b):
            here = pl.ds(pl.multiple_of(b * rows, 16), rows)
            prev = pl.ds(pl.multiple_of(lax.rem(b + blocks - 1, blocks) * rows, 16), rows)
            nxt = pl.ds(pl.multiple_of(lax.rem(b + 1, blocks) * rows, 16), rows)
            h = (dot(x[here, :], up[...]) + jnp.concatenate([up_bias[...]] * 4, axis=1)).astype(jnp.bfloat16)
            hid[here, :] = h
            a = gelu(h.astype(jnp.float32))
            low = a.astype(jnp.bfloat16)
            act[here, 3 * w : 7 * w] = low

            @pl.when(b < blocks - 1)
            def _():
                act[nxt, 0 : 3 * w] = low[:, w:]

            @pl.when(b == blocks - 1)
            def _():
                act[0:rows, 0 : 3 * w] = before(a[:, w:])

            @pl.when(b > 0)
            def _():
                act[prev, 7 * w : 10 * w] = low[:, : 3 * w]

            @pl.when(b == 0)
            def _():
                act[(blocks - 1) * rows : blocks * rows, 7 * w : 10 * w] = after(a[:, : 3 * w])

    copies[2].wait()
    section(4, x1, up2, b2_ref, hid2, act2, w2, 1)
    copies[3].wait()

    for k in range(4):
        @pl.loop(0, 2)
        def _(b):
            here = pl.ds(pl.multiple_of(b * 2 * rows, 16), 2 * rows)
            y = dot(act2[here, k * w2 : (k + 7) * w2], res2[...])
            y = (y + hid2[here, k * w2 : (k + 1) * w2].astype(jnp.float32) + rb2_ref[...]).astype(jnp.bfloat16)
            for i in range(2):
                x2[pl.ds(pl.multiple_of((b * 8 + i * 4 + k) * rows, 16), rows), :] = y[i * rows : (i + 1) * rows]

    copies[4].wait()
    section(16, x2, up3, b3_ref, hid3, act3, w3, 1)
    copies[5].wait()
    rb3 = jnp.concatenate([rb3_ref[...]] * 2, axis=1)

    @pl.loop(0, 16)
    def _(b):
        here = pl.ds(pl.multiple_of(b * rows, 16), frames)
        for k in range(2):
            y = dot(act3[here, 2 * k * w3 : (2 * k + 8) * w3], res3[...])
            y = y + hid3[here, 2 * k * w3 : (2 * k + 2) * w3].astype(jnp.float32) + rb3
            for i in range(2):
                fine[pl.ds(b * 4 + 2 * k + i, frames, stride=64), :] = y[:, i * w3 : (i + 1) * w3]

    @pl.loop(0, 16)
    def _(b):
        here = pl.ds(pl.multiple_of(b * 4 * frames, 16), 4 * frames)
        out_ref[here, :] = fine[here, :].astype(jnp.bfloat16)


def decode(lat, first, last, weights):
    (up1, b1, res1, rb1, up2, b2, res2, rb2, up3, b3, res3, rb3) = weights
    rows = lat.shape[0]
    edge = 16
    frames = rows - edge
    w1, w2, w3 = b1.shape[0], b2.shape[0], b3.shape[0]
    zero = jnp.zeros((w3, w3), res3.dtype)
    pair = jnp.concatenate(
        [jnp.concatenate([res3, zero], axis=0), jnp.concatenate([zero, res3], axis=0)], axis=1
    )
    edges = jnp.broadcast_to(
        jnp.stack([jnp.where(first, 0.0, 1.0), jnp.where(last, 0.0, 1.0)] * 4)[:, None], (8, 128)
    ).astype(jnp.float32)
    row = lambda v: v[None, :]
    vm = pl.BlockSpec(memory_space=pltpu.VMEM)
    hb = pl.BlockSpec(memory_space=pl.ANY)
    bf = jnp.bfloat16
    return pl.pallas_call(
        functools.partial(decoder_kernel, frames, edge),
        out_shape=jax.ShapeDtypeStruct((frames * 64, w3), bf),
        in_specs=[vm] * 8 + [hb] * 6,
        out_specs=vm,
        scratch_shapes=[
            pltpu.VMEM(up1.shape, bf),
            pltpu.VMEM(res1.shape, bf),
            pltpu.VMEM(up2.shape, bf),
            pltpu.VMEM(res2.shape, bf),
            pltpu.VMEM(up3.shape, bf),
            pltpu.VMEM(pair.shape, bf),
            pltpu.VMEM((rows, 10 * w1), bf),
            pltpu.VMEM((rows, 4 * w1), bf),
            pltpu.VMEM((4 * rows, w1), bf),
            pltpu.VMEM((4 * rows, 10 * w2), bf),
            pltpu.VMEM((4 * rows, 4 * w2), bf),
            pltpu.VMEM((16 * rows, w2), bf),
            pltpu.VMEM((16 * rows, 10 * w3), bf),
            pltpu.VMEM((16 * rows, 4 * w3), bf),
            pltpu.VMEM((64 * frames, w3), jnp.float32),
            pltpu.SemaphoreType.DMA((6,)),
        ],
        compiler_params=pltpu.CompilerParams(vmem_limit_bytes=60 * 1024 * 1024),
    )(lat, row(b1), row(rb1), row(b2), row(rb2), row(b3), row(rb3), edges, up1, res1, up2, res2, up3, pair)


def body(
    signal,
    gate,
    filter_taps,
    skip,
    up1_weight,
    up1_bias,
    res1_weight,
    res1_bias,
    up2_weight,
    up2_bias,
    res2_weight,
    res2_bias,
    up3_weight,
    up3_bias,
    res3_weight,
    res3_bias,
):
    parts = lax.axis_size("seq")
    frames = signal.shape[1]
    chans = signal.shape[0] // parts
    modulus = 2 * parts * frames
    source, taps = (
        lax.all_to_all(
            signal.astype(jnp.float32).astype(jnp.bfloat16),
            "seq",
            split_axis=0,
            concat_axis=1,
            tiled=True,
        ).astype(jnp.float32),
        lax.all_to_all(
            filter_taps.astype(jnp.bfloat16), "seq", split_axis=0, concat_axis=1, tiled=True
        ).astype(filter_taps.dtype),
    )
    my_skip = lax.dynamic_slice_in_dim(skip, lax.axis_index("seq") * chans, chans, 0)
    tables = (
        angle_table(2 * parts, parts, 2 * parts)
        + angle_table(2 * parts, frames, modulus)
        + angle_table(frames, frames, frames)
    )
    sig_re, sig_im = forward(source.reshape(chans, parts, frames), tables)
    fil_re, fil_im = forward(taps.reshape(chans, parts, frames), tables)
    prod_re = sig_re * fil_re - sig_im * fil_im
    prod_im = sig_re * fil_im + sig_im * fil_re
    conv = inverse(prod_re, prod_im, tables, modulus).reshape(chans, parts * frames)
    mixed = (conv + my_skip[:, None] * source).astype(jnp.bfloat16)
    arrived = lax.all_to_all(mixed, "seq", split_axis=1, concat_axis=0, tiled=True)
    latent = (gate.astype(jnp.float32) * arrived.astype(jnp.float32)).astype(jnp.bfloat16)
    count = parts
    up = [(i, i + 1) for i in range(count - 1)]
    down = [(i + 1, i) for i in range(count - 1)]
    prev = lax.ppermute(latent[:, -1], "seq", up)
    nxt = lax.ppermute(latent[:, 0], "seq", down)
    at = lax.broadcasted_iota(jnp.int32, (16, 1), 0)
    halo = jnp.where(at < 8, nxt[None, :], prev[None, :])
    lat = jnp.concatenate([latent.T, halo], axis=0)
    me = lax.axis_index("seq")
    weights = (
        up1_weight, up1_bias, res1_weight, res1_bias, up2_weight, up2_bias,
        res2_weight, res2_bias, up3_weight, up3_bias, res3_weight, res3_bias,
    )
    return decode(lat, me == 0, me == parts - 1, weights)


def solution(mesh):
    placed = (
        P(None, ("grp", "seq")),
        P(None, ("grp", "seq")),
        P(None, "seq"),
        P(),
        P(),
        P(),
        P(),
        P(),
        P(),
        P(),
        P(),
        P(),
        P(),
        P(),
        P(),
        P(),
    )
    return jax.shard_map(
        body, mesh=mesh, in_specs=placed, out_specs=P(("grp", "seq"), None), check_vma=False
    )
```

profile of v0, /device:TPU:0, one launch (start us, length us, event | category | flops | bytes accessed | tf_op | source)
XLA Modules:
  0.0 96.3 jit_solution(11744611923875793266)
XLA Ops:
  0.0 1.8 %convert_element_type.103 = bf16[1024,128]{1,0:T(8,128)(2,1)} convert(f32[1024,128]{1,0:T(8,128)} %param.18) | non-fusion elementwise | flops 131072 | bytes 786432 | tf_op jit(solution)/shard_map/convert_element_type | solution.py:242
  1.8 7.4 %all-to-all-start.1 = ((bf16[16,64,128]{2,1,0:T(8,128)(2,1)}), bf16[16,64,128]{2,1,0:T(8,128)(2,1)S(1)}, u32[]{:S(2)}, u32[]{:S(2)}) async-start(bf16[16,64,128]{2,1,0:T(8,128)(2,1)} %bitcast.8), calls=%async_computation.1 | async-start | bytes 524288 | tf_op jit(solution)/shard_map/all_to_all | solution.py:241
  9.1 0.8 dynamic_slice.3
  9.9 0.1 fusion.89
  10.0 9.2 %all-to-all-done.1 = bf16[16,64,128]{2,1,0:T(8,128)(2,1)S(1)} async-done(((bf16[16,64,128]{2,1,0:T(8,128)(2,1)}), bf16[16,64,128]{2,1,0:T(8,128)(2,1)S(1)}, u32[]{:S(2)}, u32[]{:S(2)}) %all-to-all-start.1) | async-done | bytes 262176 | tf_op jit(solution)/shard_map/all_to_all | solution.py:241
  19.2 3.5 %all-to-all-start = ((bf16[16,64,128]{2,1,0:T(8,128)(2,1)}), bf16[16,64,128]{2,1,0:T(8,128)(2,1)S(1)}, u32[]{:S(2)}, u32[]{:S(2)}) async-start(bf16[16,64,128]{2,1,0:T(8,128)(2,1)} %bitcast.101), calls=%async_computation | async-start | bytes 524288 | tf_op jit(solution)/shard_map/all_to_all | solution.py:234
  22.7 0.7 convolution_negate_fusion
  23.4 0.7 fusion.31
  24.1 2.2 %fusion.8 = f32[64,32,128]{2,1,0:T(8,128)} fusion(f32[32,64,128]{2,0,1:T(8,128)S(1)} %convolution_negate_fusion, f32[32,64,128]{2,0,1:T(8,128)S(1)} %fusion.31, f32[32,128]{1,0:T(8,128)S(1)} %get-tuple-element.9, f32[32,128]{1,0:T(8,128)S(1)} %get-tuple-element.10), kind=kOutput, calls=%fused_computation.19 | convolution fusion | flops 403668992 | bytes 3178496 | tf_op jit(solution)/shard_map/ckm,mj->ckj/dot_general | solution.py:30
  26.3 1.2 %fusion.4 = f32[64,32,128]{2,1,0:T(8,128)S(1)} fusion(f32[32,64,128]{2,0,1:T(8,128)S(1)} %fusion.31, f32[32,64,128]{2,0,1:T(8,128)S(1)} %convolution_negate_fusion, f32[32,128]{1,0:T(8,128)S(1)} %get-tuple-element.9, f32[32,128]{1,0:T(8,128)S(1)} %get-tuple-element.10), kind=kOutput, calls=%fused_computation.15 | convolution fusion | flops 403668992 | bytes 3178496 | tf_op jit(solution)/shard_map/ckm,mj->ckj/dot_general | solution.py:33
  27.5 5.2 %all-to-all-done = bf16[16,64,128]{2,1,0:T(8,128)(2,1)S(1)} async-done(((bf16[16,64,128]{2,1,0:T(8,128)(2,1)}), bf16[16,64,128]{2,1,0:T(8,128)(2,1)S(1)}, u32[]{:S(2)}, u32[]{:S(2)}) %all-to-all-start) | async-done | bytes 262176 | tf_op jit(solution)/shard_map/all_to_all | solution.py:234
  32.7 0.7 convolution_negate_fusion.1
  33.4 0.7 fusion.34
  34.1 1.2 %fusion.14 = f32[64,32,128]{2,1,0:T(8,128)S(1)} fusion(f32[32,64,128]{2,0,1:T(8,128)S(1)} %convolution_negate_fusion.1, f32[32,64,128]{2,0,1:T(8,128)S(1)} %fusion.34, f32[32,128]{1,0:T(8,128)S(1)} %get-tuple-element.9, f32[32,128]{1,0:T(8,128)S(1)} %get-tuple-element.10), kind=kOutput, calls=%fused_computation.25 | convolution fusion | flops 403668992 | bytes 3178496 | tf_op jit(solution)/shard_map/ckm,mj->ckj/dot_general | solution.py:30
  35.3 0.0 copy-start
  35.4 1.2 %fusion.10 = f32[64,32,128]{2,1,0:T(8,128)S(1)} fusion(f32[32,64,128]{2,0,1:T(8,128)S(1)} %fusion.34, f32[32,64,128]{2,0,1:T(8,128)S(1)} %convolution_negate_fusion.1, f32[32,128]{1,0:T(8,128)S(1)} %get-tuple-element.9, f32[32,128]{1,0:T(8,128)S(1)} %get-tuple-element.10), kind=kOutput, calls=%fused_computation.21 | convolution fusion | flops 403668992 | bytes 3178496 | tf_op jit(solution)/shard_map/ckm,mj->ckj/dot_general | solution.py:33
  36.6 1.3 %convolution_add_fusion.2 = f32[64,32,128]{2,1,0:T(8,128)S(1)} fusion(f32[64,32,128]{2,1,0:T(8,128)S(1)} %fusion.14, f32[32,64,128]{2,0,1:T(8,128)S(1)} %fusion.34, f32[32,64,128]{2,0,1:T(8,128)S(1)} %convolution_negate_fusion.1, f32[32,128]{1,0:T(8,128)S(1)} %get-tuple-element.9, f32[32,128]{1,0:T(8,128)S(1)} %get-tuple-element.10), kind=kOutput, calls=%fused_computation.6 | convolution fusion | flops 403931136 | bytes 4227072 | tf_op jit(solution)/shard_map/ckm,mj->ckj/dot_general | solution.py:30
  37.9 0.0 copy-done
  37.9 1.3 %convolution_add_fusion.1 = f32[64,32,128]{2,1,0:T(8,128)S(1)} fusion(f32[64,32,128]{2,1,0:T(8,128)S(1)} %copy-done, f32[32,64,128]{2,0,1:T(8,128)S(1)} %fusion.31, f32[32,64,128]{2,0,1:T(8,128)S(1)} %convolution_negate_fusion, f32[32,128]{1,0:T(8,128)S(1)} %get-tuple-element.9, f32[32,128]{1,0:T(8,128)S(1)} %get-tuple-element.10), kind=kOutput, calls=%fused_computation.4 | convolution fusion | flops 403931136 | bytes 4227072 | tf_op jit(solution)/shard_map/ckm,mj->ckj/dot_general | solution.py:30
  39.1 1.3 %convolution_subtract_fusion.1 = f32[64,32,128]{2,1,0:T(8,128)S(1)} fusion(f32[64,32,128]{2,1,0:T(8,128)S(1)} %fusion.4, f32[32,64,128]{2,0,1:T(8,128)S(1)} %convolution_negate_fusion, f32[32,64,128]{2,0,1:T(8,128)S(1)} %fusion.31, f32[32,128]{1,0:T(8,128)S(1)} %get-tuple-element.9, f32[32,128]{1,0:T(8,128)S(1)} %get-tuple-element.10), kind=kOutput, calls=%fused_computation.2 | convolution fusion | flops 403931136 | bytes 4227072 | tf_op jit(solution)/shard_map/ckm,mj->ckj/dot_general | solution.py:33
  40.4 1.6 %multiply_subtract_fusion = (f32[64,32,128]{2,1,0:T(8,128)S(1)}, f32[64,32,128]{2,1,0:T(8,128)S(1)}) fusion(f32[64,32,128]{2,1,0:T(8,128)S(1)} %convolution_subtract_fusion.1, f32[64,32,128]{2,1,0:T(8,128)S(1)} %convolution_add_fusion.2, f32[64,32,128]{2,1,0:T(8,128)S(1)} %convolution_add_fusion.1, f32[64,32,128]{2,1,0:T(8,128)S(1)} %fusion.10, ...), kind=kOutput, calls=%fused_computation.35 | convolution fusion | flops 405504000 | bytes 8421376 | tf_op jit(solution)/shard_map/ckm,mj->ckj/dot_general | solution.py:33
  42.1 1.2 %fusion.51 = f32[64,32,128]{2,1,0:T(8,128)S(1)} fusion(f32[64,32,128]{2,1,0:T(8,128)S(1)} %get-tuple-element.7), kind=kOutput, calls=%fused_computation.73 | convolution fusion | flops 402882560 | bytes 2097152 | tf_op jit(solution)/shard_map/ckm,mj->ckj/dot_general | solution.py:41
  43.3 1.2 %fusion.49 = f32[64,32,128]{2,1,0:T(8,128)S(1)} fusion(f32[64,32,128]{2,1,0:T(8,128)S(1)} %get-tuple-element.8), kind=kOutput, calls=%fused_computation.71 | convolution fusion | flops 402882560 | bytes 2097152 | tf_op jit(solution)/shard_map/ckm,mj->ckj/dot_general | solution.py:44
  44.5 1.2 %convolution_subtract_fusion = f32[64,32,128]{2,1,0:T(8,128)S(1)} fusion(f32[64,32,128]{2,1,0:T(8,128)S(1)} %fusion.51, f32[64,32,128]{2,1,0:T(8,128)S(1)} %get-tuple-element.8), kind=kOutput, calls=%fused_computation.1 | convolution fusion | flops 403144704 | bytes 3145728 | tf_op jit(solution)/shard_map/ckm,mj->ckj/dot_general | solution.py:41
  45.7 1.2 %convolution_add_fusion = f32[64,32,128]{2,1,0:T(8,128)S(1)} fusion(f32[64,32,128]{2,1,0:T(8,128)S(1)} %fusion.49, f32[64,32,128]{2,1,0:T(8,128)S(1)} %get-tuple-element.7), kind=kOutput, calls=%fused_computation | convolution fusion | flops 403144704 | bytes 3145728 | tf_op jit(solution)/shard_map/ckm,mj->ckj/dot_general | solution.py:44
  47.0 0.0 copy-start.1
  47.0 0.0 copy-start.2
  47.0 0.8 fusion.19
  47.8 1.0 fusion.3
  48.8 0.8 copy.27
  49.6 3.5 %all-to-all-start.2 = ((bf16[64,16,128]{2,0,1:T(8,128)(2,1)}), bf16[64,16,128]{2,0,1:T(8,128)(2,1)S(1)}, u32[]{:S(2)}, u32[]{:S(2)}) async-start(bf16[64,16,128]{2,0,1:T(8,128)(2,1)} %copy.27), calls=%async_computation.2 | async-start | bytes 524288 | tf_op jit(solution)/shard_map/all_to_all | solution.py:257
  53.1 0.0 copy-done.1
  53.1 0.1 copy.24
  53.3 0.0 copy-done.2
  53.3 0.8 fusion.25.res3_hbm
  54.1 9.0 %all-to-all-done.2 = bf16[64,16,128]{2,0,1:T(8,128)(2,1)S(1)} async-done(((bf16[64,16,128]{2,0,1:T(8,128)(2,1)}), bf16[64,16,128]{2,0,1:T(8,128)(2,1)S(1)}, u32[]{:S(2)}, u32[]{:S(2)}) %all-to-all-start.2) | async-done | bytes 262176 | tf_op jit(solution)/shard_map/all_to_all | solution.py:257
  63.2 0.2 copy.28
  63.4 0.1 multiply_convert_fusion
  63.5 1.3 %collective-permute-start = (bf16[1024]{0:T(1024)(128)(2,1)S(1)}, bf16[1024]{0:T(1024)(128)(2,1)S(1)}, u32[]{:S(2)}, u32[]{:S(2)}) collective-permute-start(bf16[1024]{0:T(1024)(128)(2,1)S(1)} %get-tuple-element.5), channel_id=1, source_target_pairs={{1,0},{2,1},{3,2},{4,3},{5,4},{6,5},{7,6},{8,7},{9,8},{10,9},{11,1... | collective-permute-start | bytes 6152 | tf_op jit(solution)/shard_map/ppermute | solution.py:263
  64.8 3.0 %collective-permute-start.1 = (bf16[1024]{0:T(1024)(128)(2,1)S(1)}, bf16[1024]{0:T(1024)(128)(2,1)S(1)}, u32[]{:S(2)}, u32[]{:S(2)}) collective-permute-start(bf16[1024]{0:T(1024)(128)(2,1)S(1)} %get-tuple-element.6), channel_id=1, source_target_pairs={{0,1},{1,2},{2,3},{3,4},{4,5},{5,6},{6,7},{7,8},{8,9},{9,10},{10,1... | collective-permute-start | bytes 6152 | tf_op jit(solution)/shard_map/ppermute | solution.py:262
  67.8 0.1 stack.8
  67.9 0.0 collective-permute-done
  67.9 0.7 collective-permute-done.1
  68.6 0.1 broadcast_select_fusion
  68.7 0.7 pad_maximum_fusion.lat_ref
  69.4 0.7 broadcast_in_dim.73.edges_ref
  70.1 26.1 %shard_map.154 = bf16[8192,128]{1,0:T(8,128)(2,1)} custom-call(bf16[144,1024]{1,0:T(8,128)(2,1)} %pad_maximum_fusion.lat_ref, f32[1,512]{1,0:T(1,128)} %bitcast.102, f32[1,512]{1,0:T(1,128)} %bitcast.103, f32[1,256]{1,0:T(1,128)} %bitcast.104, f32[1,256]{1,0:T(1,128)} %bitcast.105, f32[1,128]{1,0:T(1,128)} %bitcast.106, f32[1,128]{1,0:T(1,128)} %bitcast.107, ...), custom_call_target="tpu_custom_call" | custom-call | tf_op jit(solution)/shard_map/pallas_call | solution.py:184
  (3 shorter events, 0.1 us)
Async XLA Ops:
  1.8 17.4 %all-to-all-start.1 = ((bf16[16,64,128]{2,1,0:T(8,128)(2,1)}), bf16[16,64,128]{2,1,0:T(8,128)(2,1)S(1)}, u32[]{:S(2)}, u32[]{:S(2)}) async-start(bf16[16,64,128]{2,1,0:T(8,128)(2,1)} %bitcast.8), calls=%async_computation.1 | async-start | bytes 524288 | tf_op jit(solution)/shard_map/all_to_all | solution.py:241
  19.2 13.5 %all-to-all-start = ((bf16[16,64,128]{2,1,0:T(8,128)(2,1)}), bf16[16,64,128]{2,1,0:T(8,128)(2,1)S(1)}, u32[]{:S(2)}, u32[]{:S(2)}) async-start(bf16[16,64,128]{2,1,0:T(8,128)(2,1)} %bitcast.101), calls=%async_computation | async-start | bytes 524288 | tf_op jit(solution)/shard_map/all_to_all | solution.py:234
  35.3 2.5 %copy-start = (f32[64,32,128]{2,1,0:T(8,128)S(1)}, f32[64,32,128]{2,1,0:T(8,128)}, u32[]{:S(2)}) copy-start(f32[64,32,128]{2,1,0:T(8,128)} %fusion.8) | copy-start | bytes 3145732
  47.0 6.1 %copy-start.1 = (bf16[1024,128]{1,0:T(8,128)(2,1)S(1)}, bf16[1024,128]{1,0:T(8,128)(2,1)}, u32[]{:S(2)}) copy-start(bf16[1024,128]{1,0:T(8,128)(2,1)} %param.17) | copy-start | bytes 786436
  47.0 6.3 %copy-start.2 = (bf16[896,128]{1,0:T(8,128)(2,1)S(1)}, bf16[896,128]{1,0:T(8,128)(2,1)}, u32[]{:S(2)}) copy-start(bf16[896,128]{1,0:T(8,128)(2,1)} %param.30) | copy-start | bytes 688132
  49.6 13.5 %all-to-all-start.2 = ((bf16[64,16,128]{2,0,1:T(8,128)(2,1)}), bf16[64,16,128]{2,0,1:T(8,128)(2,1)S(1)}, u32[]{:S(2)}, u32[]{:S(2)}) async-start(bf16[64,16,128]{2,0,1:T(8,128)(2,1)} %copy.27), calls=%async_computation.2 | async-start | bytes 524288 | tf_op jit(solution)/shard_map/all_to_all | solution.py:257
  63.5 4.5 %collective-permute-start = (bf16[1024]{0:T(1024)(128)(2,1)S(1)}, bf16[1024]{0:T(1024)(128)(2,1)S(1)}, u32[]{:S(2)}, u32[]{:S(2)}) collective-permute-start(bf16[1024]{0:T(1024)(128)(2,1)S(1)} %get-tuple-element.5), channel_id=1, source_target_pairs={{1,0},{2,1},{3,2},{4,3},{5,4},{6,5},{7,6},{8,7},{9,8},{10,9},{11,1... | collective-permute-start | bytes 6152 | tf_op jit(solution)/shard_map/ppermute | solution.py:263
  64.8 3.8 %collective-permute-start.1 = (bf16[1024]{0:T(1024)(128)(2,1)S(1)}, bf16[1024]{0:T(1024)(128)(2,1)S(1)}, u32[]{:S(2)}, u32[]{:S(2)}) collective-permute-start(bf16[1024]{0:T(1024)(128)(2,1)S(1)} %get-tuple-element.6), channel_id=1, source_target_pairs={{0,1},{1,2},{2,3},{3,4},{4,5},{5,6},{6,7},{7,8},{8,9},{9,10},{10,1... | collective-permute-start | bytes 6152 | tf_op jit(solution)/shard_map/ppermute | solution.py:262
where the time goes:
time: 98 us; the launch traced here: 96.3 us
  Pallas kernels  26.1 us (27%)
  waiting for transfers between devices  24.1 us (25%)
  matrix products  20.7 us (21%)
  starting transfers between devices  18.7 us (19%)
  other arithmetic  3.6 us (4%)
  local copies, waits for them, and re-layouts  2.67 us (3%)
    pallas_call x1, Pallas kernels, decode(): pl.pallas_call(functools.partial(decoder_kernel, frames, edge), out_shape...  26.1 us
    all_to_all x1, waiting for transfers between devices, body(): lax.all_to_all(filter_taps.astype(jnp.bfloat16), 'seq', split_axis=0, con...  9.19 us
    all_to_all x1, waiting for transfers between devices, body(): lax.all_to_all(mixed, 'seq', split_axis=1, concat_axis=0, tiled=True)  8.99 us
    all_to_all x1, starting transfers between devices, body(): lax.all_to_all(filter_taps.astype(jnp.bfloat16), 'seq', split_axis=0, con...  7.36 us
    all_to_all x1, waiting for transfers between devices, body(): lax.all_to_all(signal.astype(jnp.float32).astype(jnp.bfloat16), 'seq', sp...  5.2 us
    all_to_all x1, starting transfers between devices, body(): lax.all_to_all(signal.astype(jnp.float32).astype(jnp.bfloat16), 'seq', sp...  3.53 us
    all_to_all x1, starting transfers between devices, body(): lax.all_to_all(mixed, 'seq', split_axis=1, concat_axis=0, tiled=True)  3.53 us
    dot_general x2, matrix products, forward(): jnp.einsum('ckm,mj->ckj', turned_re, inner_cos, precision=HIGHEST)  3.43 us
  transfers between devices with their start and end apart: 5, of which 4 were waited for; matrix products, arithmetic and copies ran while one was open for 7% of the time, Pallas kernels for 0%

commit v1 on v0

--- a/solution.py
+++ b/solution.py
@@ -208,6 +208,226 @@
     )(lat, row(b1), row(rb1), row(b2), row(rb2), row(b3), row(rb3), edges, up1, res1, up2, res2, up3, pair)
 
 
+def mix_kernel(
+    groups, parts, nc, sig_ref, gate_ref, tap_ref, lat_ref,
+    sig_in, tap_in, mix_out, mix_in, tap_wide, sig_wide, mix_wide, line, edge_next, edge_prev,
+    sig_send, sig_recv, tap_send, tap_recv, mix_send, mix_recv, edge_send, edge_recv,
+):
+    g, s = lax.axis_index("grp"), lax.axis_index("seq")
+    total = groups * parts
+    me = g * parts + s
+    frames = sig_ref.shape[1]
+
+    def place(index):
+        return (index // parts, lax.rem(index, parts))
+
+    def rows(index):
+        return pl.ds(pl.multiple_of(index * nc, 16), nc)
+
+    def sig_copy(peer, slot):
+        return pltpu.make_async_remote_copy(
+            sig_ref.at[rows(peer)], sig_in.at[rows(slot)], sig_send.at[peer], sig_recv.at[slot],
+            device_id=place(peer), device_id_type=pl.DeviceIdType.MESH,
+        )
+
+    def tap_copy(peer, slot):
+        return pltpu.make_async_remote_copy(
+            tap_ref.at[rows(g * parts + peer)], tap_in.at[rows(slot)], tap_send.at[peer], tap_recv.at[slot],
+            device_id=(g, peer), device_id_type=pl.DeviceIdType.MESH,
+        )
+
+    def mix_copy(peer, slot):
+        return pltpu.make_async_remote_copy(
+            mix_out.at[rows(peer)], mix_in.at[rows(slot)], mix_send.at[peer], mix_recv.at[slot],
+            device_id=place(peer), device_id_type=pl.DeviceIdType.MESH,
+        )
+
+    barrier = pltpu.get_barrier_semaphore()
+
+    @pl.loop(1, total)
+    def _(step):
+        pl.semaphore_signal(
+            barrier, inc=1, device_id=place(lax.rem(me + step, total)), device_id_type=pl.DeviceIdType.MESH
+        )
+
+    pl.semaphore_wait(barrier, total - 1)
+
+    @pl.loop(1, parts)
+    def _(step):
+        tap_copy(lax.rem(s + step, parts), s).start()
+
+    @pl.loop(1, total)
+    def _(step):
+        sig_copy(lax.rem(me + step, total), me).start()
+
+    sig_in[rows(me), :] = sig_ref[rows(me), :]
+    tap_in[rows(s), :] = tap_ref[rows(me), :]
+    line[...] = jnp.zeros_like(line)
+
+    @pl.loop(1, parts)
+    def _(step):
+        tap_copy(s, lax.rem(s + step, parts)).wait_recv()
+
+    tap_wide[...] = tap_in[...].astype(jnp.float32)
+
+    @pl.loop(1, total)
+    def _(step):
+        sig_copy(me, lax.rem(me + step, total)).wait_recv()
+
+    sig_wide[...] = sig_in[...].astype(jnp.float32)
+    below = lax.broadcasted_iota(jnp.int32, (frames, frames), 1) >= lax.broadcasted_iota(
+        jnp.int32, (frames, frames), 0
+    )
+
+    @pl.loop(0, nc)
+    def _(c):
+        for part in range(groups):
+            line[(2 * part + 1) * parts : (2 * part + 2) * parts, :] = sig_wide[
+                pl.ds(part * parts * nc + c, parts, stride=nc), :
+            ]
+        acc = jnp.zeros((total, frames), jnp.float32)
+        last = jnp.zeros((frames, frames), jnp.float32)
+        for pair in range(0, parts, 2):
+            tiles, shifted = [], []
+            for d in (pair, pair + 1):
+                row = tap_wide[pl.ds(d * nc + c, 1), :]
+                turned = pltpu.roll(jnp.broadcast_to(row, (frames, frames)), 0, 1, stride=1, stride_axis=0)
+                tiles.append(jnp.where(below, turned, last).astype(jnp.bfloat16))
+                last = turned
+                shifted.append(
+                    jnp.concatenate(
+                        [
+                            line[(2 * part + 1) * parts - d : (2 * part + 2) * parts - d, :]
+                            for part in range(groups)
+                        ],
+                        axis=0,
+                    ).astype(jnp.bfloat16)
+                )
+            acc = acc + jnp.dot(
+                jnp.concatenate(shifted, axis=1),
+                jnp.concatenate(tiles, axis=0),
+                preferred_element_type=jnp.float32,
+            )
+        mix_wide[pl.ds(c, total, stride=nc), :] = acc
+
+    mix_out[...] = mix_wide[...].astype(jnp.bfloat16)
+
+    @pl.loop(1, total)
+    def _(step):
+        mix_copy(lax.rem(me + step, total), me).start()
+
+    mix_in[rows(me), :] = mix_out[rows(me), :]
+
+    @pl.loop(1, total)
+    def _(step):
+        mix_copy(me, lax.rem(me + step, total)).wait_recv()
+
+    latent = mix_in[...].astype(jnp.float32) * gate_ref[...].astype(jnp.float32)
+    lat_ref[0:frames, :] = latent.T.astype(jnp.bfloat16)
+
+    nxt, prv = lax.rem(s + 1, parts), lax.rem(s + parts - 1, parts)
+    down = pltpu.make_async_remote_copy(
+        lat_ref.at[pl.ds(0, 16)], edge_next, edge_send.at[0], edge_recv.at[0],
+        device_id=(g, prv), device_id_type=pl.DeviceIdType.MESH,
+    )
+    up = pltpu.make_async_remote_copy(
+        lat_ref.at[pl.ds(frames - 16, 16)], edge_prev, edge_send.at[1], edge_recv.at[1],
+        device_id=(g, nxt), device_id_type=pl.DeviceIdType.MESH,
+    )
+    down.start()
+    up.start()
+
+    @pl.loop(1, parts)
+    def _(step):
+        tap_copy(lax.rem(s + step, parts), s).wait_send()
+
+    @pl.loop(1, total)
+    def _(step):
+        sig_copy(lax.rem(me + step, total), me).wait_send()
+        mix_copy(lax.rem(me + step, total), me).wait_send()
+
+    down.wait()
+    up.wait()
+    at = lax.broadcasted_iota(jnp.int32, (16, 1), 0)
+    lat_ref[frames : frames + 16, :] = jnp.where(
+        at < 8, edge_next[...].astype(jnp.float32), edge_prev[...].astype(jnp.float32)
+    ).astype(jnp.bfloat16)
+
+
+def mix(signal, gate, taps, groups, parts):
+    chans, frames = signal.shape
+    total = groups * parts
+    nc = chans // total
+    vm = pl.BlockSpec(memory_space=pltpu.VMEM)
+    bf, f32 = jnp.bfloat16, jnp.float32
+    dma = pltpu.SemaphoreType.DMA
+    return pl.pallas_call(
+        functools.partial(mix_kernel, groups, parts, nc),
+        out_shape=jax.ShapeDtypeStruct((frames + 16, chans), bf),
+        in_specs=[vm] * 3,
+        out_specs=vm,
+        scratch_shapes=[
+            pltpu.VMEM((chans, frames), bf),
+            pltpu.VMEM((parts * nc, frames), bf),
+            pltpu.VMEM((chans, frames), bf),
+            pltpu.VMEM((chans, frames), bf),
+            pltpu.VMEM((parts * nc, frames), f32),
+            pltpu.VMEM((chans, frames), f32),
+            pltpu.VMEM((chans, frames), f32),
+            pltpu.VMEM((groups * 2 * parts, frames), f32),
+            pltpu.VMEM((16, chans), bf),
+            pltpu.VMEM((16, chans), bf),
+            dma((total,)), dma((total,)), dma((parts,)), dma((parts,)),
+            dma((total,)), dma((total,)), dma((2,)), dma((2,)),
+        ],
+        compiler_params=pltpu.CompilerParams(
+            collective_id=0, has_side_effects=True, vmem_limit_bytes=40 * 1024 * 1024
+        ),
+    )(signal, gate, taps)
+
+
+def transformed(signal, gate, filter_taps, skip):
+    parts = lax.axis_size("seq")
+    frames = signal.shape[1]
+    chans = signal.shape[0] // parts
+    modulus = 2 * parts * frames
+    source, taps = (
+        lax.all_to_all(
+            signal.astype(jnp.float32).astype(jnp.bfloat16),
+            "seq",
+            split_axis=0,
+            concat_axis=1,
+            tiled=True,
+        ).astype(jnp.float32),
+        lax.all_to_all(
+            filter_taps.astype(jnp.bfloat16), "seq", split_axis=0, concat_axis=1, tiled=True
+        ).astype(filter_taps.dtype),
+    )
+    my_skip = lax.dynamic_slice_in_dim(skip, lax.axis_index("seq") * chans, chans, 0)
+    tables = (
+        angle_table(2 * parts, parts, 2 * parts)
+        + angle_table(2 * parts, frames, modulus)
+        + angle_table(frames, frames, frames)
+    )
+    sig_re, sig_im = forward(source.reshape(chans, parts, frames), tables)
+    fil_re, fil_im = forward(taps.reshape(chans, parts, frames), tables)
+    prod_re = sig_re * fil_re - sig_im * fil_im
+    prod_im = sig_re * fil_im + sig_im * fil_re
+    conv = inverse(prod_re, prod_im, tables, modulus).reshape(chans, parts * frames)
+    mixed = (conv + my_skip[:, None] * source).astype(jnp.bfloat16)
+    arrived = lax.all_to_all(mixed, "seq", split_axis=1, concat_axis=0, tiled=True)
+    latent = (gate.astype(jnp.float32) * arrived.astype(jnp.float32)).astype(jnp.bfloat16)
+    count = parts
+    up = [(i, i + 1) for i in range(count - 1)]
+    down = [(i + 1, i) for i in range(count - 1)]
+    prev = lax.ppermute(latent[:, -1], "seq", up)
+    nxt = lax.ppermute(latent[:, 0], "seq", down)
+    at = lax.broadcasted_iota(jnp.int32, (16, 1), 0)
+    halo = jnp.where(at < 8, nxt[None, :], prev[None, :])
+    lat = jnp.concatenate([latent.T, halo], axis=0)
+    return lat
+
+
 def body(
     signal,
     gate,
@@ -226,44 +446,14 @@
     res3_weight,
     res3_bias,
 ):
-    parts = lax.axis_size("seq")
-    frames = signal.shape[1]
-    chans = signal.shape[0] // parts
-    modulus = 2 * parts * frames
-    source, taps = (
-        lax.all_to_all(
-            signal.astype(jnp.float32).astype(jnp.bfloat16),
-            "seq",
-            split_axis=0,
-            concat_axis=1,
-            tiled=True,
-        ).astype(jnp.float32),
-        lax.all_to_all(
-            filter_taps.astype(jnp.bfloat16), "seq", split_axis=0, concat_axis=1, tiled=True
-        ).astype(filter_taps.dtype),
-    )
-    my_skip = lax.dynamic_slice_in_dim(skip, lax.axis_index("seq") * chans, chans, 0)
-    tables = (
-        angle_table(2 * parts, parts, 2 * parts)
-        + angle_table(2 * parts, frames, modulus)
-        + angle_table(frames, frames, frames)
-    )
-    sig_re, sig_im = forward(source.reshape(chans, parts, frames), tables)
-    fil_re, fil_im = forward(taps.reshape(chans, parts, frames), tables)
-    prod_re = sig_re * fil_re - sig_im * fil_im
-    prod_im = sig_re * fil_im + sig_im * fil_re
-    conv = inverse(prod_re, prod_im, tables, modulus).reshape(chans, parts * frames)
-    mixed = (conv + my_skip[:, None] * source).astype(jnp.bfloat16)
-    arrived = lax.all_to_all(mixed, "seq", split_axis=1, concat_axis=0, tiled=True)
-    latent = (gate.astype(jnp.float32) * arrived.astype(jnp.float32)).astype(jnp.bfloat16)
-    count = parts
-    up = [(i, i + 1) for i in range(count - 1)]
-    down = [(i + 1, i) for i in range(count - 1)]
-    prev = lax.ppermute(latent[:, -1], "seq", up)
-    nxt = lax.ppermute(latent[:, 0], "seq", down)
-    at = lax.broadcasted_iota(jnp.int32, (16, 1), 0)
-    halo = jnp.where(at < 8, nxt[None, :], prev[None, :])
-    lat = jnp.concatenate([latent.T, halo], axis=0)
+    parts, groups = lax.axis_size("seq"), lax.axis_size("grp")
+    chans, frames = signal.shape
+    if frames == 128 and parts % 2 == 0 and chans % (groups * parts * 16) == 0:
+        first_lag = (lax.broadcasted_iota(jnp.int32, (1, frames), 1) == 0) & (lax.axis_index("seq") == 0)
+        taps = (filter_taps + jnp.where(first_lag, skip[:, None], 0.0)).astype(jnp.bfloat16)
+        lat = mix(signal, gate, taps, groups, parts)
+    else:
+        lat = transformed(signal, gate, filter_taps, skip)
     me = lax.axis_index("seq")
     weights = (
         up1_weight, up1_bias, res1_weight, res1_bias, up2_weight, up2_bias,

time: 98 us -> 75.2 us (0.77); the launches traced: 96.3 us -> 74.9 us
  Pallas kernels: 26.1 us -> 68.4 us
  waiting for transfers between devices: 24.1 us -> 0 us
  matrix products: 20.7 us -> 0 us
  starting transfers between devices: 18.7 us -> 0 us
    pallas_call x0 -> x1, Pallas kernels: none -> 42.3 us  [mix(): pl.pallas_call(functools.partial(mix_kernel, groups, parts, nc), out_shap...]
    all_to_all x3 -> x0, waiting for transfers between devices: 23.4 us -> none  [the longest x1 9.19 us: body(): lax.all_to_all(filter_taps.astype(jnp.bfloat16), 'seq', split_axis=0, con...]
    dot_general x18 -> x0, matrix products: 20.7 us -> none  [the longest x2 3.43 us: forward(): jnp.einsum('ckm,mj->ckj', turned_re, inner_cos, precision=HIGHEST)]
    all_to_all x3 -> x0, starting transfers between devices: 14.4 us -> none  [the longest x1 7.36 us: body(): lax.all_to_all(filter_taps.astype(jnp.bfloat16), 'seq', split_axis=0, con...]
    ppermute x2 -> x0, starting transfers between devices: 4.32 us -> none  [the longest x1 3.03 us: body(): prev = lax.ppermute(latent[:, -1], 'seq', up)]
    unnamed x7 -> x6, local copies, waits for them, and re-layouts: 0.16 us -> 2.59 us
    concatenate x1, other arithmetic: 0.84 us -> 1.89 us  [decode(): jnp.concatenate([jnp.concatenate([res3, zero], axis=0), jnp.concatenate([...]
  transfers between devices with their start and end apart: 5 -> 0, of which waited for: 4 -> 0; matrix products, arithmetic and copies ran while one was open for 7% -> 0% of each run, Pallas kernels for 0% -> 0%
where the time goes in v1:
time: 75.2 us; the launch traced here: 74.9 us
  Pallas kernels  68.4 us (91%)
  local copies, waits for them, and re-layouts  3.34 us (4%)
  other arithmetic  3.14 us (4%)
    pallas_call x1, Pallas kernels, mix(): pl.pallas_call(functools.partial(mix_kernel, groups, parts, nc), out_shap...  42.3 us
    pallas_call x1, Pallas kernels, decode(): pl.pallas_call(functools.partial(decoder_kernel, frames, edge), out_shape...  26.1 us
    unnamed x6, local copies, waits for them, and re-layouts  2.59 us
    concatenate x1, other arithmetic, decode(): jnp.concatenate([jnp.concatenate([res3, zero], axis=0), jnp.concatenate([...  1.89 us

profile of v1, /device:TPU:0, one launch (start us, length us, event | category | flops | bytes accessed | tf_op | source)
XLA Modules:
  0.0 74.9 jit_solution(8290713497528459220)
XLA Ops:
  0.0 0.1 stack.8
  0.1 0.7 broadcast_in_dim.55.edges_ref
  0.8 1.2 %add_convert_fusion.tap_ref = bf16[1024,128]{1,0:T(8,128)(2,1)S(1)} fusion(f32[1024,128]{1,0:T(8,128)} %param.18, f32[1024]{0:T(1024)} %param.19, pred[128]{0:T(512)(128)(4,1)S(1)} %compare_and_fusion), kind=kLoop, calls=%fused_computation.5 | loop fusion | flops 393216 | bytes 790656 | tf_op jit(solution)/shard_map/convert_element_type | solution.py:453
  2.0 0.0 copy-start.1
  2.0 0.9 %copy-done.1 = bf16[1024,128]{1,0:T(8,128)(2,1)S(1)} copy-done((bf16[1024,128]{1,0:T(8,128)(2,1)S(1)}, bf16[1024,128]{1,0:T(8,128)(2,1)}, u32[]{:S(2)}) %copy-start.1) | copy-done | bytes 262168
  3.0 0.0 copy-start.2
  3.0 0.9 %copy-done.2 = bf16[1024,128]{1,0:T(8,128)(2,1)S(1)} copy-done((bf16[1024,128]{1,0:T(8,128)(2,1)S(1)}, bf16[1024,128]{1,0:T(8,128)(2,1)}, u32[]{:S(2)}) %copy-start.2) | copy-done | bytes 262168
  3.9 42.3 %shard_map.154.lat_ref = bf16[144,1024]{1,0:T(8,128)(2,1)S(1)} custom-call(bf16[1024,128]{1,0:T(8,128)(2,1)S(1)} %copy-done.1, bf16[1024,128]{1,0:T(8,128)(2,1)S(1)} %copy-done.2, bf16[1024,128]{1,0:T(8,128)(2,1)S(1)} %add_convert_fusion.tap_ref), custom_call_target="tpu_custom_call" | custom-call | tf_op jit(solution)/shard_map/pallas_call | solution.py:364
  46.2 0.0 copy-start
  46.2 0.7 copy-done
  46.9 1.9 %fusion.2.res3_hbm = bf16[1024,256]{1,0:T(8,128)(2,1)} fusion(bf16[896,128]{1,0:T(8,128)(2,1)} %param.30), kind=kLoop, calls=%fused_computation.4 | loop fusion | flops 2097152 | bytes 753664 | tf_op jit(solution)/shard_map/concatenate | solution.py:174
  48.8 26.1 %shard_map.155 = bf16[8192,128]{1,0:T(8,128)(2,1)} custom-call(bf16[144,1024]{1,0:T(8,128)(2,1)} %copy-done, f32[1,512]{1,0:T(1,128)} %bitcast.8, f32[1,512]{1,0:T(1,128)} %bitcast.9, f32[1,256]{1,0:T(1,128)} %bitcast.10, f32[1,256]{1,0:T(1,128)} %bitcast.11, f32[1,128]{1,0:T(1,128)} %bitcast.12, f32[1,128]{1,0:T(1,128)} %bitcast.13, ...), custom_call_target="tpu_custom_call" | custom-call | tf_op jit(solution)/shard_map/pallas_call | solution.py:184
  (1 shorter events, 0.0 us)
Async XLA Ops:
  2.0 1.0 %copy-start.1 = (bf16[1024,128]{1,0:T(8,128)(2,1)S(1)}, bf16[1024,128]{1,0:T(8,128)(2,1)}, u32[]{:S(2)}) copy-start(bf16[1024,128]{1,0:T(8,128)(2,1)} %sig_ref.1) | copy-start | bytes 786436
  3.0 0.9 %copy-start.2 = (bf16[1024,128]{1,0:T(8,128)(2,1)S(1)}, bf16[1024,128]{1,0:T(8,128)(2,1)}, u32[]{:S(2)}) copy-start(bf16[1024,128]{1,0:T(8,128)(2,1)} %gate_ref.1) | copy-start | bytes 786436
  46.2 0.7 copy-start

commit v2 on v1

--- a/solution.py
+++ b/solution.py
@@ -57,24 +57,35 @@
 
 
 def decoder_kernel(
-    frames, edge, lat_ref, b1_ref, rb1_ref, b2_ref, rb2_ref, b3_ref, rb3_ref, edges_ref,
+    frames, edge, lat_ref, b1_ref, rb1_ref, b2_ref, rb2_ref, b3_ref, rb3_ref,
     up1_hbm, res1_hbm, up2_hbm, res2_hbm, up3_hbm, res3_hbm,
     out_ref,
     up1, res1, up2, res2, up3, res3, act1, hid1, x1, act2, hid2, x2, act3, hid3, fine, sems,
 ):
+    w1, w2, w3 = b1_ref.shape[1], b2_ref.shape[1], b3_ref.shape[1]
     copies = [
         pltpu.make_async_copy(src, dst, sems.at[i])
         for i, (src, dst) in enumerate(
-            [(up1_hbm, up1), (res1_hbm, res1), (up2_hbm, up2), (res2_hbm, res2), (up3_hbm, up3), (res3_hbm, res3)]
+            [
+                (up1_hbm, up1),
+                (res1_hbm, res1),
+                (up2_hbm, up2),
+                (res2_hbm, res2),
+                (up3_hbm, up3),
+                (res3_hbm, res3.at[pl.ds(0, 7 * w3), pl.ds(0, w3)]),
+                (res3_hbm, res3.at[pl.ds(w3, 7 * w3), pl.ds(w3, w3)]),
+            ]
         )
     ]
     for copy in copies:
         copy.start()
+    res3[7 * w3 : 8 * w3, 0:w3] = jnp.zeros((w3, w3), res3.dtype)
+    res3[0:w3, w3 : 2 * w3] = jnp.zeros((w3, w3), res3.dtype)
     rows = frames + edge
-    w1, w2, w3 = b1_ref.shape[1], b2_ref.shape[1], b3_ref.shape[1]
     at = lax.broadcasted_iota(jnp.int32, (rows, 1), 0)
-    keep_first = edges_ref[0:1, 0:1]
-    keep_last = edges_ref[1:2, 0:1]
+    me, parts = lax.axis_index("seq"), lax.axis_size("seq")
+    keep_first = jnp.where(me == 0, 0.0, 1.0)
+    keep_last = jnp.where(me == parts - 1, 0.0, 1.0)
     before_scale = jnp.where(at == 0, keep_first, 1.0)
     after_scale = jnp.where(at == frames - 1, keep_last, 1.0)
 
@@ -147,6 +158,7 @@
     copies[4].wait()
     section(16, x2, up3, b3_ref, hid3, act3, w3, 1)
     copies[5].wait()
+    copies[6].wait()
     rb3 = jnp.concatenate([rb3_ref[...]] * 2, axis=1)
 
     @pl.loop(0, 16)
@@ -164,19 +176,12 @@
         out_ref[here, :] = fine[here, :].astype(jnp.bfloat16)
 
 
-def decode(lat, first, last, weights):
+def decode(lat, weights):
     (up1, b1, res1, rb1, up2, b2, res2, rb2, up3, b3, res3, rb3) = weights
     rows = lat.shape[0]
     edge = 16
     frames = rows - edge
     w1, w2, w3 = b1.shape[0], b2.shape[0], b3.shape[0]
-    zero = jnp.zeros((w3, w3), res3.dtype)
-    pair = jnp.concatenate(
-        [jnp.concatenate([res3, zero], axis=0), jnp.concatenate([zero, res3], axis=0)], axis=1
-    )
-    edges = jnp.broadcast_to(
-        jnp.stack([jnp.where(first, 0.0, 1.0), jnp.where(last, 0.0, 1.0)] * 4)[:, None], (8, 128)
-    ).astype(jnp.float32)
     row = lambda v: v[None, :]
     vm = pl.BlockSpec(memory_space=pltpu.VMEM)
     hb = pl.BlockSpec(memory_space=pl.ANY)
@@ -184,7 +189,7 @@
     return pl.pallas_call(
         functools.partial(decoder_kernel, frames, edge),
         out_shape=jax.ShapeDtypeStruct((frames * 64, w3), bf),
-        in_specs=[vm] * 8 + [hb] * 6,
+        in_specs=[vm] * 7 + [hb] * 6,
         out_specs=vm,
         scratch_shapes=[
             pltpu.VMEM(up1.shape, bf),
@@ -192,7 +197,7 @@
             pltpu.VMEM(up2.shape, bf),
             pltpu.VMEM(res2.shape, bf),
             pltpu.VMEM(up3.shape, bf),
-            pltpu.VMEM(pair.shape, bf),
+            pltpu.VMEM((8 * w3, 2 * w3), bf),
             pltpu.VMEM((rows, 10 * w1), bf),
             pltpu.VMEM((rows, 4 * w1), bf),
             pltpu.VMEM((4 * rows, w1), bf),
@@ -202,16 +207,19 @@
             pltpu.VMEM((16 * rows, 10 * w3), bf),
             pltpu.VMEM((16 * rows, 4 * w3), bf),
             pltpu.VMEM((64 * frames, w3), jnp.float32),
-            pltpu.SemaphoreType.DMA((6,)),
+            pltpu.SemaphoreType.DMA((7,)),
         ],
         compiler_params=pltpu.CompilerParams(vmem_limit_bytes=60 * 1024 * 1024),
-    )(lat, row(b1), row(rb1), row(b2), row(rb2), row(b3), row(rb3), edges, up1, res1, up2, res2, up3, pair)
+    )(lat, row(b1), row(rb1), row(b2), row(rb2), row(b3), row(rb3), up1, res1, up2, res2, up3, res3)
+
+
+CHUNKS = 2
 
 
 def mix_kernel(
-    groups, parts, nc, sig_ref, gate_ref, tap_ref, lat_ref,
+    groups, parts, nc, sig_ref, gate_hbm, tap_ref, lat_ref, gate_ref,
     sig_in, tap_in, mix_out, mix_in, tap_wide, sig_wide, mix_wide, line, edge_next, edge_prev,
-    sig_send, sig_recv, tap_send, tap_recv, mix_send, mix_recv, edge_send, edge_recv,
+    sig_send, sig_recv, tap_send, tap_recv, mix_send, mix_recv, edge_send, edge_recv, own_sem,
 ):
     g, s = lax.axis_index("grp"), lax.axis_index("seq")
     total = groups * parts
@@ -221,27 +229,42 @@
     def place(index):
         return (index // parts, lax.rem(index, parts))
 
-    def rows(index):
-        return pl.ds(pl.multiple_of(index * nc, 16), nc)
-
-    def sig_copy(peer, slot):
+    half = nc // CHUNKS
+
+    def rows(index, q):
+        return pl.ds(pl.multiple_of(index * nc + q * half, 16), half)
+
+    def slots(index, q, count):
+        return pl.ds(pl.multiple_of((q * count + index) * half, 16), half)
+
+    def sig_copy(peer, slot, q):
         return pltpu.make_async_remote_copy(
-            sig_ref.at[rows(peer)], sig_in.at[rows(slot)], sig_send.at[peer], sig_recv.at[slot],
+            sig_ref.at[rows(peer, q)], sig_in.at[slots(slot, q, total)],
+            sig_send.at[q * total + peer], sig_recv.at[q * total + slot],
             device_id=place(peer), device_id_type=pl.DeviceIdType.MESH,
         )
 
-    def tap_copy(peer, slot):
+    def tap_copy(peer, slot, q):
         return pltpu.make_async_remote_copy(
-            tap_ref.at[rows(g * parts + peer)], tap_in.at[rows(slot)], tap_send.at[peer], tap_recv.at[slot],
+            tap_ref.at[rows(g * parts + peer, q)], tap_in.at[slots(slot, q, parts)],
+            tap_send.at[q * parts + peer], tap_recv.at[q * parts + slot],
             device_id=(g, peer), device_id_type=pl.DeviceIdType.MESH,
         )
 
-    def mix_copy(peer, slot):
+    def mix_copy(peer, slot, q):
         return pltpu.make_async_remote_copy(
-            mix_out.at[rows(peer)], mix_in.at[rows(slot)], mix_send.at[peer], mix_recv.at[slot],
+            mix_out.at[slots(peer, q, total)], mix_in.at[rows(slot, q)],
+            mix_send.at[q * total + peer], mix_recv.at[q * total + slot],
             device_id=place(peer), device_id_type=pl.DeviceIdType.MESH,
         )
 
+    own = [pltpu.make_async_copy(gate_hbm, gate_ref, own_sem.at[CHUNKS])]
+    for q in range(CHUNKS):
+        own.append(
+            pltpu.make_async_copy(sig_ref.at[rows(me, q)], sig_in.at[slots(me, q, total)], own_sem.at[q])
+        )
+    for copy in own:
+        copy.start()
     barrier = pltpu.get_barrier_semaphore()
 
     @pl.loop(1, total)
@@ -252,75 +275,82 @@
 
     pl.semaphore_wait(barrier, total - 1)
 
-    @pl.loop(1, parts)
-    def _(step):
-        tap_copy(lax.rem(s + step, parts), s).start()
-
-    @pl.loop(1, total)
-    def _(step):
-        sig_copy(lax.rem(me + step, total), me).start()
-
-    sig_in[rows(me), :] = sig_ref[rows(me), :]
-    tap_in[rows(s), :] = tap_ref[rows(me), :]
+    for q in range(CHUNKS):
+        @pl.loop(1, parts)
+        def _(step):
+            tap_copy(lax.rem(s + step, parts), s, q).start()
+
+        @pl.loop(1, total)
+        def _(step):
+            sig_copy(lax.rem(me + step, total), me, q).start()
+
+        tap_in[slots(s, q, parts), :] = tap_ref[rows(me, q), :]
+
     line[...] = jnp.zeros_like(line)
-
-    @pl.loop(1, parts)
-    def _(step):
-        tap_copy(s, lax.rem(s + step, parts)).wait_recv()
-
-    tap_wide[...] = tap_in[...].astype(jnp.float32)
-
-    @pl.loop(1, total)
-    def _(step):
-        sig_copy(me, lax.rem(me + step, total)).wait_recv()
-
-    sig_wide[...] = sig_in[...].astype(jnp.float32)
     below = lax.broadcasted_iota(jnp.int32, (frames, frames), 1) >= lax.broadcasted_iota(
         jnp.int32, (frames, frames), 0
     )
 
-    @pl.loop(0, nc)
-    def _(c):
-        for part in range(groups):
-            line[(2 * part + 1) * parts : (2 * part + 2) * parts, :] = sig_wide[
-                pl.ds(part * parts * nc + c, parts, stride=nc), :
-            ]
-        acc = jnp.zeros((total, frames), jnp.float32)
-        last = jnp.zeros((frames, frames), jnp.float32)
-        for pair in range(0, parts, 2):
-            tiles, shifted = [], []
-            for d in (pair, pair + 1):
-                row = tap_wide[pl.ds(d * nc + c, 1), :]
-                turned = pltpu.roll(jnp.broadcast_to(row, (frames, frames)), 0, 1, stride=1, stride_axis=0)
-                tiles.append(jnp.where(below, turned, last).astype(jnp.bfloat16))
-                last = turned
-                shifted.append(
-                    jnp.concatenate(
-                        [
-                            line[(2 * part + 1) * parts - d : (2 * part + 2) * parts - d, :]
-                            for part in range(groups)
-                        ],
-                        axis=0,
-                    ).astype(jnp.bfloat16)
+    for q in range(CHUNKS):
+        @pl.loop(1, parts)
+        def _(step):
+            tap_copy(s, lax.rem(s + step, parts), q).wait_recv()
+
+        few = slice(q * parts * half, (q + 1) * parts * half)
+        tap_wide[few, :] = tap_in[few, :].astype(jnp.float32)
+        own[1 + q].wait()
+
+        @pl.loop(1, total)
+        def _(step):
+            sig_copy(me, lax.rem(me + step, total), q).wait_recv()
+
+        many = slice(q * total * half, (q + 1) * total * half)
+        sig_wide[many, :] = sig_in[many, :].astype(jnp.float32)
+
+        @pl.loop(0, half)
+        def _(c):
+            for part in range(groups):
+                line[(2 * part + 1) * parts : (2 * part + 2) * parts, :] = sig_wide[
+                    pl.ds((q * total + part * parts) * half + c, parts, stride=half), :
+                ]
+            acc = jnp.zeros((total, frames), jnp.float32)
+            last = jnp.zeros((frames, frames), jnp.float32)
+            for pair in range(0, parts, 2):
+                tiles, shifted = [], []
+                for d in (pair, pair + 1):
+                    row = tap_wide[pl.ds((q * parts + d) * half + c, 1), :]
+                    turned = pltpu.roll(jnp.broadcast_to(row, (frames, frames)), 0, 1, stride=1, stride_axis=0)
+                    tiles.append(jnp.where(below, turned, last).astype(jnp.bfloat16))
+                    last = turned
+                    shifted.append(
+                        jnp.concatenate(
+                            [
+                                line[(2 * part + 1) * parts - d : (2 * part + 2) * parts - d, :]
+                                for part in range(groups)
+                            ],
+                            axis=0,
+                        ).astype(jnp.bfloat16)
+                    )
+                acc = acc + jnp.dot(
+                    jnp.concatenate(shifted, axis=1),
+                    jnp.concatenate(tiles, axis=0),
+                    preferred_element_type=jnp.float32,
                 )
-            acc = acc + jnp.dot(
-                jnp.concatenate(shifted, axis=1),
-                jnp.concatenate(tiles, axis=0),
-                preferred_element_type=jnp.float32,
-            )
-        mix_wide[pl.ds(c, total, stride=nc), :] = acc
-
-    mix_out[...] = mix_wide[...].astype(jnp.bfloat16)
-
-    @pl.loop(1, total)
-    def _(step):
-        mix_copy(lax.rem(me + step, total), me).start()
-
-    mix_in[rows(me), :] = mix_out[rows(me), :]
-
-    @pl.loop(1, total)
-    def _(step):
-        mix_copy(me, lax.rem(me + step, total)).wait_recv()
+            mix_wide[pl.ds(q * total * half + c, total, stride=half), :] = acc
+
+        mix_out[many, :] = mix_wide[many, :].astype(jnp.bfloat16)
+
+        @pl.loop(1, total)
+        def _(step):
+            mix_copy(lax.rem(me + step, total), me, q).start()
+
+        mix_in[rows(me, q), :] = mix_out[slots(me, q, total), :]
+
+    own[0].wait()
+    for q in range(CHUNKS):
+        @pl.loop(1, total)
+        def _(step):
+            mix_copy(me, lax.rem(me + step, total), q).wait_recv()
 
     latent = mix_in[...].astype(jnp.float32) * gate_ref[...].astype(jnp.float32)
     lat_ref[0:frames, :] = latent.T.astype(jnp.bfloat16)
@@ -337,14 +367,15 @@
     down.start()
     up.start()
 
-    @pl.loop(1, parts)
-    def _(step):
-        tap_copy(lax.rem(s + step, parts), s).wait_send()
-
-    @pl.loop(1, total)
-    def _(step):
-        sig_copy(lax.rem(me + step, total), me).wait_send()
-        mix_copy(lax.rem(me + step, total), me).wait_send()
+    for q in range(CHUNKS):
+        @pl.loop(1, parts)
+        def _(step):
+            tap_copy(lax.rem(s + step, parts), s, q).wait_send()
+
+        @pl.loop(1, total)
+        def _(step):
+            sig_copy(lax.rem(me + step, total), me, q).wait_send()
+            mix_copy(lax.rem(me + step, total), me, q).wait_send()
 
     down.wait()
     up.wait()
@@ -358,15 +389,17 @@
     chans, frames = signal.shape
     total = groups * parts
     nc = chans // total
+    hb = pl.BlockSpec(memory_space=pl.ANY)
     vm = pl.BlockSpec(memory_space=pltpu.VMEM)
     bf, f32 = jnp.bfloat16, jnp.float32
     dma = pltpu.SemaphoreType.DMA
     return pl.pallas_call(
         functools.partial(mix_kernel, groups, parts, nc),
         out_shape=jax.ShapeDtypeStruct((frames + 16, chans), bf),
-        in_specs=[vm] * 3,
+        in_specs=[hb, hb, vm],
         out_specs=vm,
         scratch_shapes=[
+            pltpu.VMEM((chans, frames), bf),
             pltpu.VMEM((chans, frames), bf),
             pltpu.VMEM((parts * nc, frames), bf),
             pltpu.VMEM((chans, frames), bf),
@@ -377,8 +410,8 @@
             pltpu.VMEM((groups * 2 * parts, frames), f32),
             pltpu.VMEM((16, chans), bf),
             pltpu.VMEM((16, chans), bf),
-            dma((total,)), dma((total,)), dma((parts,)), dma((parts,)),
-            dma((total,)), dma((total,)), dma((2,)), dma((2,)),
+            dma((CHUNKS * total,)), dma((CHUNKS * total,)), dma((CHUNKS * parts,)), dma((CHUNKS * parts,)),
+            dma((CHUNKS * total,)), dma((CHUNKS * total,)), dma((2,)), dma((2,)), dma((CHUNKS + 1,)),
         ],
         compiler_params=pltpu.CompilerParams(
             collective_id=0, has_side_effects=True, vmem_limit_bytes=40 * 1024 * 1024
@@ -448,18 +481,17 @@
 ):
     parts, groups = lax.axis_size("seq"), lax.axis_size("grp")
     chans, frames = signal.shape
-    if frames == 128 and parts % 2 == 0 and chans % (groups * parts * 16) == 0:
+    if frames == 128 and parts % 2 == 0 and chans % (groups * parts * 16 * CHUNKS) == 0:
         first_lag = (lax.broadcasted_iota(jnp.int32, (1, frames), 1) == 0) & (lax.axis_index("seq") == 0)
         taps = (filter_taps + jnp.where(first_lag, skip[:, None], 0.0)).astype(jnp.bfloat16)
         lat = mix(signal, gate, taps, groups, parts)
     else:
         lat = transformed(signal, gate, filter_taps, skip)
-    me = lax.axis_index("seq")
     weights = (
         up1_weight, up1_bias, res1_weight, res1_bias, up2_weight, up2_bias,
         res2_weight, res2_bias, up3_weight, up3_bias, res3_weight, res3_bias,
     )
-    return decode(lat, me == 0, me == parts - 1, weights)
+    return decode(lat, weights)
 
 
 def solution(mesh):

time: 75.2 us -> 70.3 us (0.935)
  Pallas kernels: 68.4 us -> 66.3 us
  other arithmetic: 3.14 us -> 1.25 us
    pallas_call x1, Pallas kernels: 42.3 us -> 40.3 us  [mix(): pl.pallas_call(functools.partial(mix_kernel, groups, parts, nc), out_shap...]
    concatenate x1 -> x0, other arithmetic: 1.89 us -> none  [decode(): jnp.concatenate([jnp.concatenate([res3, zero], axis=0), jnp.concatenate([...]
where the time goes in v2:
time: 70.3 us; the launch traced here: 70.1 us
  Pallas kernels  66.3 us (94%)
  local copies, waits for them, and re-layouts  2.59 us (4%)
  other arithmetic  1.25 us (2%)
    pallas_call x1, Pallas kernels, mix(): pl.pallas_call(functools.partial(mix_kernel, groups, parts, nc), out_shap...  40.3 us
    pallas_call x1, Pallas kernels, decode(): pl.pallas_call(functools.partial(decoder_kernel, frames, edge), out_shape...  26 us
    unnamed x6, local copies, waits for them, and re-layouts  2.59 us

profile of v2, /device:TPU:0, one launch (start us, length us, event | category | flops | bytes accessed | tf_op | source)
XLA Modules:
  0.0 70.1 jit_solution(2113525120517056596)
XLA Ops:
  0.0 1.2 %add_convert_fusion.tap_ref = bf16[1024,128]{1,0:T(8,128)(2,1)S(1)} fusion(f32[1024,128]{1,0:T(8,128)} %param.18, f32[1024]{0:T(1024)} %param.19, pred[128]{0:T(512)(128)(4,1)S(1)} %compare_and_fusion), kind=kLoop, calls=%fused_computation | loop fusion | flops 393216 | bytes 790656 | tf_op jit(solution)/shard_map/convert_element_type | solution.py:486
  1.3 0.0 copy-start.1
  1.3 0.9 %copy-done.1 = bf16[1024,128]{1,0:T(8,128)(2,1)S(1)} copy-done((bf16[1024,128]{1,0:T(8,128)(2,1)S(1)}, bf16[1024,128]{1,0:T(8,128)(2,1)}, u32[]{:S(2)}) %copy-start.1) | copy-done | bytes 262168
  2.2 0.0 copy-start.2
  2.2 0.9 %copy-done.2 = bf16[1024,128]{1,0:T(8,128)(2,1)S(1)} copy-done((bf16[1024,128]{1,0:T(8,128)(2,1)S(1)}, bf16[1024,128]{1,0:T(8,128)(2,1)}, u32[]{:S(2)}) %copy-start.2) | copy-done | bytes 262168
  3.2 40.3 %shard_map.154.lat_ref = bf16[144,1024]{1,0:T(8,128)(2,1)S(1)} custom-call(bf16[1024,128]{1,0:T(8,128)(2,1)S(1)} %copy-done.1, bf16[1024,128]{1,0:T(8,128)(2,1)S(1)} %copy-done.2, bf16[1024,128]{1,0:T(8,128)(2,1)S(1)} %add_convert_fusion.tap_ref), custom_call_target="tpu_custom_call" | custom-call | tf_op jit(solution)/shard_map/pallas_call | solution.py:396
  43.4 0.0 copy-start
  43.5 0.7 copy-done
  44.1 26.0 %shard_map.155 = bf16[8192,128]{1,0:T(8,128)(2,1)} custom-call(bf16[144,1024]{1,0:T(8,128)(2,1)} %copy-done, f32[1,512]{1,0:T(1,128)} %bitcast.6, f32[1,512]{1,0:T(1,128)} %bitcast.7, f32[1,256]{1,0:T(1,128)} %bitcast.8, f32[1,256]{1,0:T(1,128)} %bitcast.9, f32[1,128]{1,0:T(1,128)} %bitcast.10, f32[1,128]{1,0:T(1,128)} %bitcast.11, ...), custom_call_target="tpu_custom_call" | custom-call | tf_op jit(solution)/shard_map/pallas_call | solution.py:189
  (1 shorter events, 0.0 us)
Async XLA Ops:
  1.3 1.0 %copy-start.1 = (bf16[1024,128]{1,0:T(8,128)(2,1)S(1)}, bf16[1024,128]{1,0:T(8,128)(2,1)}, u32[]{:S(2)}) copy-start(bf16[1024,128]{1,0:T(8,128)(2,1)} %sig_ref.1) | copy-start | bytes 786436
  2.2 0.9 %copy-start.2 = (bf16[1024,128]{1,0:T(8,128)(2,1)S(1)}, bf16[1024,128]{1,0:T(8,128)(2,1)}, u32[]{:S(2)}) copy-start(bf16[1024,128]{1,0:T(8,128)(2,1)} %gate_hbm.1) | copy-start | bytes 786436
  43.4 0.7 %copy-start = (bf16[144,1024]{1,0:T(8,128)(2,1)}, bf16[144,1024]{1,0:T(8,128)(2,1)S(1)}, u32[]{:S(2)}) copy-start(bf16[144,1024]{1,0:T(8,128)(2,1)S(1)} %shard_map.154.lat_ref) | copy-start | bytes 884740

commit v3 on v2

--- a/solution.py
+++ b/solution.py
@@ -115,7 +115,7 @@
         x1[k * rows : (k + 1) * rows, :] = y.astype(jnp.bfloat16)
 
     def section(blocks, x, up, up_bias, hid, act, w, group):
-        @pl.loop(0, blocks)
+        @pl.loop(0, blocks, unroll=2)
         def _(b):
             here = pl.ds(pl.multiple_of(b * rows, 16), rows)
             prev = pl.ds(pl.multiple_of(lax.rem(b + blocks - 1, blocks) * rows, 16), rows)
@@ -126,21 +126,12 @@
             low = a.astype(jnp.bfloat16)
             act[here, 3 * w : 7 * w] = low
 
-            @pl.when(b < blocks - 1)
-            def _():
-                act[nxt, 0 : 3 * w] = low[:, w:]
-
-            @pl.when(b == blocks - 1)
-            def _():
-                act[0:rows, 0 : 3 * w] = before(a[:, w:])
-
-            @pl.when(b > 0)
-            def _():
-                act[prev, 7 * w : 10 * w] = low[:, : 3 * w]
-
-            @pl.when(b == 0)
-            def _():
-                act[(blocks - 1) * rows : blocks * rows, 7 * w : 10 * w] = after(a[:, : 3 * w])
+            act[nxt, 0 : 3 * w] = low[:, w:]
+            act[prev, 7 * w : 10 * w] = low[:, : 3 * w]
+
+        end = slice((blocks - 1) * rows, blocks * rows)
+        act[0:rows, 0 : 3 * w] = before(act[end, 4 * w : 7 * w].astype(jnp.float32))
+        act[end, 7 * w : 10 * w] = after(act[0:rows, 3 * w : 6 * w].astype(jnp.float32))
 
     copies[2].wait()
     section(4, x1, up2, b2_ref, hid2, act2, w2, 1)
@@ -161,7 +152,7 @@
     copies[6].wait()
     rb3 = jnp.concatenate([rb3_ref[...]] * 2, axis=1)
 
-    @pl.loop(0, 16)
+    @pl.loop(0, 16, unroll=2)
     def _(b):
         here = pl.ds(pl.multiple_of(b * rows, 16), frames)
         for k in range(2):
@@ -170,7 +161,7 @@
             for i in range(2):
                 fine[pl.ds(b * 4 + 2 * k + i, frames, stride=64), :] = y[:, i * w3 : (i + 1) * w3]
 
-    @pl.loop(0, 16)
+    @pl.loop(0, 16, unroll=2)
     def _(b):
         here = pl.ds(pl.multiple_of(b * 4 * frames, 16), 4 * frames)
         out_ref[here, :] = fine[here, :].astype(jnp.bfloat16)
@@ -414,7 +405,7 @@
             dma((CHUNKS * total,)), dma((CHUNKS * total,)), dma((2,)), dma((2,)), dma((CHUNKS + 1,)),
         ],
         compiler_params=pltpu.CompilerParams(
-            collective_id=0, has_side_effects=True, vmem_limit_bytes=40 * 1024 * 1024
+            collective_id=0, has_side_effects=True, vmem_limit_bytes=60 * 1024 * 1024
         ),
     )(signal, gate, taps)
 

time: 70.3 us -> 66.3 us (0.943)
  local copies, waits for them, and re-layouts: 2.59 us -> 0 us
  Pallas kernels: 66.3 us -> 64.2 us
  other arithmetic: 1.25 us -> 1.96 us
    pallas_call x1, Pallas kernels: 26 us -> 22.5 us  [decode(): pl.pallas_call(functools.partial(decoder_kernel, frames, edge), out_shape...]
    unnamed x6 -> x0, local copies, waits for them, and re-layouts: 2.59 us -> none
    pallas_call x1, Pallas kernels: 40.3 us -> 41.7 us  [mix(): pl.pallas_call(functools.partial(mix_kernel, groups, parts, nc), out_shap...]
    convert_element_type x1, other arithmetic: 1.24 us -> 1.95 us  [body(): (filter_taps + jnp.where(first_lag, skip[:, None], 0.0)).astype(jnp.bfloa...]
where the time goes in v3:
time: 66.3 us; the launch traced here: 66.2 us
  Pallas kernels  64.2 us (97%)
  other arithmetic  1.96 us (3%)
    pallas_call x1, Pallas kernels, mix(): pl.pallas_call(functools.partial(mix_kernel, groups, parts, nc), out_shap...  41.7 us
    pallas_call x1, Pallas kernels, decode(): pl.pallas_call(functools.partial(decoder_kernel, frames, edge), out_shape...  22.5 us
    convert_element_type x1, other arithmetic, body(): (filter_taps + jnp.where(first_lag, skip[:, None], 0.0)).astype(jnp.bfloa...  1.95 us

profile of v3, /device:TPU:0, one launch (start us, length us, event | category | flops | bytes accessed | tf_op | source)
XLA Modules:
  0.0 66.2 jit_solution(17633086118079996215)
XLA Ops:
  0.0 1.9 %add_convert_fusion.tap_ref = bf16[1024,128]{1,0:T(8,128)(2,1)} fusion(f32[1024,128]{1,0:T(8,128)} %param.18, f32[1024]{0:T(1024)} %param.19, pred[128]{0:T(512)(128)(4,1)S(1)} %compare_and_fusion), kind=kLoop, calls=%fused_computation | loop fusion | flops 393216 | bytes 790656 | tf_op jit(solution)/shard_map/convert_element_type | solution.py:477
  2.0 41.7 %shard_map.154.lat_ref = bf16[144,1024]{1,0:T(8,128)(2,1)} custom-call(bf16[1024,128]{1,0:T(8,128)(2,1)} %sig_ref.1, bf16[1024,128]{1,0:T(8,128)(2,1)} %gate_hbm.1, bf16[1024,128]{1,0:T(8,128)(2,1)} %add_convert_fusion.tap_ref), custom_call_target="tpu_custom_call" | custom-call | tf_op jit(solution)/shard_map/pallas_call | solution.py:387
  43.6 22.5 %shard_map.155 = bf16[8192,128]{1,0:T(8,128)(2,1)} custom-call(bf16[144,1024]{1,0:T(8,128)(2,1)} %shard_map.154.lat_ref, f32[1,512]{1,0:T(1,128)} %bitcast.6, f32[1,512]{1,0:T(1,128)} %bitcast.7, f32[1,256]{1,0:T(1,128)} %bitcast.8, f32[1,256]{1,0:T(1,128)} %bitcast.9, f32[1,128]{1,0:T(1,128)} %bitcast.10, f32[1,128]{1,0:T(1,128)} %bitcast.11, ...), custom_call_target="tpu_custom_call" | custom-call | tf_op jit(solution)/shard_map/pallas_call | solution.py:180
  (1 shorter events, 0.0 us)
